TPU v7x, 512 devices: a whole 4x4x16 slice. The times are simulated.
512 devices in a mesh: node: 16 (over x, y_hi, core), rep: 32 (over z, y_lo).
Axes of the slice: x: 4, y: 4 (y_hi: 2, y_lo: 2; y = y_hi * 2 + y_lo), z: 16, core: 2. Of those that a mesh axis runs over, the one named last changes fastest.
Arguments:
- tokens: bfloat16 [65536, 16384], P(('node', 'rep')), may hold values from -6 to 6
- cotangent: bfloat16 [65536, 256], P(('node', 'rep')), may hold values from -0.08984375 to 0.08984375
- weight: bfloat16 [16384, 256], P('node'), may hold values from -0.046875 to 0.046875
- gain: bfloat16 [16384], replicated, may hold values from 0.5 to 2
- exponents: int32 [16, 32, 2, 16384], P('node', 'rep'), may hold values from -13 to -8
Outputs:
- grad_weight: float32 [16384, 256], P(('node', 'rep'))
- grad_gain: float32 [16384], P(('node', 'rep'))
Inputs may be any that keep to these rules, and one draw needn't show every extreme that they name: Integer exponents.
All inputs are finite; a program needn't handle non-finite values.
Results may differ from a plain program's by a relative error of at most 0.004.
Values may be sent and summed in bfloat16 or wider, within the bound.
A program may use at most 192 MiB of HBM per device.

v0:
```python
import jax
import jax.numpy as jnp
from jax import lax
from jax.sharding import PartitionSpec as P

EPSILON = 1e-05
SATURATE = 448.0


def powers_of_two(exponents):
    upward = jnp.left_shift(jnp.ones_like(exponents), -exponents).astype(jnp.float32)
    return (upward, 1.0 / upward)


def body(tokens, cotangent, weight, gain, exponents):
    node_count = lax.axis_size("node")
    width = tokens.shape[1]
    kv_width = cotangent.shape[1]
    block_count = exponents.shape[2]
    block_width = kv_width // block_count
    slab = width // node_count
    widened = tokens.astype(jnp.float32)
    inverse_rms = lax.rsqrt(jnp.mean(widened * widened, axis=1) + EPSILON)
    to_wire, from_wire = powers_of_two(exponents[0, 0])
    normed = (widened * inverse_rms[:, None] * gain.astype(jnp.float32)[None, :]).astype(
        jnp.bfloat16
    )

    def quantize(block_index):
        first = block_index * slab
        feature_cols = lax.dynamic_slice_in_dim(normed, first, slab, 1)
        partial_value = lax.dot_general(
            feature_cols, cotangent, (((0,), (0,)), ((), ())), preferred_element_type=jnp.float32
        )
        factor = lax.dynamic_slice_in_dim(to_wire, first, slab, 1)
        scaled = partial_value.reshape(slab, block_count, block_width) * factor.T[:, :, None]
        return jnp.clip(scaled, -SATURATE, SATURATE).astype(jnp.bfloat16).reshape(slab, kv_width)

    quantized = lax.map(quantize, jnp.arange(node_count, dtype=jnp.int32))
    back_blocks = (
        from_wire.reshape(block_count, node_count, slab).transpose(1, 0, 2).astype(jnp.bfloat16)
    )
    arrived, arrived_scales = (
        lax.all_to_all(quantized, "node", split_axis=0, concat_axis=0, tiled=True),
        lax.all_to_all(back_blocks, "node", split_axis=0, concat_axis=0, tiled=True),
    )
    restored = arrived.astype(jnp.float32).reshape(node_count, slab, block_count, block_width)
    restored = restored * arrived_scales.astype(jnp.float32).transpose(0, 2, 1)[:, :, :, None]
    node_total = jnp.sum(restored, axis=0).reshape(slab, kv_width)
    projected = lax.dot_general(
        cotangent,
        lax.all_gather(weight, "node", axis=0, tiled=True),
        (((1,), (1,)), ((), ())),
        preferred_element_type=jnp.float32,
    )
    feature_cols = widened * inverse_rms[:, None]
    full_gain = jnp.sum(projected * feature_cols, axis=0)
    grad_gain = lax.psum_scatter(full_gain, ("node", "rep"), scatter_dimension=0, tiled=True)
    grad_weight = lax.psum_scatter(node_total, "rep", scatter_dimension=0, tiled=True)
    return (grad_weight, grad_gain)


def solution(mesh):
    placed = (
        P(("node", "rep"), None),
        P(("node", "rep"), None),
        P("node", None),
        P(),
        P("node", "rep", None, None),
    )
    return jax.shard_map(
        body,
        mesh=mesh,
        in_specs=placed,
        out_specs=(P(("node", "rep"), None), P(("node", "rep"))),
        check_vma=False,
    )
```

profile of v0, /device:TPU:8, one launch (start us, length us, event | category | flops | bytes accessed | tf_op | source)
XLA Modules:
  0.0 624.3 jit_solution(5894193459120802074)
XLA Ops:
  10.5 6.1 all-to-all-start.1
  16.6 3.1 fusion.8
  20.5 5.2 fusion.7
  25.8 77.1 %while.10 = (s32[]{:T(128)}, bf16[16,1024,256]{2,1,0:T(8,128)(2,1)}, s32[16]{0:T(128)S(1)}, bf16[128,16384]{1,0:T(8,128)(2,1)}, bf16[128,256]{1,0:T(8,128)(2,1)S...) while((s32[]{:T(128)}, bf16[16,1024,256]{2,1,0:T(8,128)(2,1)}, ...), condition=%wide.region_2.3_spmd, body=%wide.region_1.2_spmd.sunk | while | flops 67895304 | bytes 2990259 | solution.py:39
  28.5 2.1 fusion.19
  32.1 1.2 mul.102
  33.3 2.1 fusion.19
  36.9 1.2 mul.102
  38.2 2.1 fusion.19
  41.7 1.2 mul.102
  43.0 2.1 fusion.19
  47.8 2.1 fusion.19
  52.6 2.1 fusion.19
  57.4 2.1 fusion.19
  62.2 2.1 fusion.19
  67.0 2.2 fusion.19
  71.9 2.1 fusion.19
  76.7 2.1 fusion.19
  81.5 2.1 fusion.19
  86.3 2.1 fusion.19
  91.2 2.1 fusion.19
  96.0 2.1 fusion.19
  100.8 2.1 fusion.19
  102.9 7.3 %all-to-all-start = ((bf16[16,1024,256]{2,1,0:T(8,128)(2,1)}), bf16[16,1024,256]{2,1,0:T(8,128)(2,1)}, u32[]{:S(2)}, u32[]{:S(2)}) async-start(bf16[16,1024,256]{2,1,0:T(8,128)(2,1)} %get-tuple-element.34), calls=%async_computation | async-start | bytes 16777216 | tf_op jit(solution)/shard_map/all_to_all | solution.py:44
  110.2 4.6 copy.16
  114.9 23.7 %mul.60 = f32[16,1024,2,128]{3,2,1,0:T(2,128)} broadcast(f32[16,1024,2]{2,1,0:T(8,128)} %copy.16), dimensions={0,1,2} | broadcast | bytes 16908288 | tf_op jit(solution)/shard_map/mul | solution.py:48
  138.6 21.6 %mul.61 = f32[16,1024,256]{2,1,0:T(8,128)} reshape(f32[16,1024,2,128]{3,2,1,0:T(2,128)} %mul.60) | data formatting | bytes 33554432 | tf_op jit(solution)/shard_map/mul | solution.py:48
  160.2 8.1 %fusion.9 = f32[16384]{0:T(1024)} fusion(f32[128]{0:T(128)S(1)} %add_rsqrt_fusion, bf16[128,16384]{1,0:T(8,128)(2,1)} %param.7, bf16[128,256]{1,0:T(8,128)(2,1)S(1)} %get-tuple-element.127, bf16[16384,256]{1,0:T(8,128)(2,1)} %all-gather.2.cloned.1.call-done), kind=kOutput, calls=%fused_computation.15 | convolution fusion | flops 1082114048 | bytes 12714496 | tf_op jit(solution)/shard_map/dot_general | solution.py:50
  168.3 74.1 %all-to-all-done = bf16[16,1024,256]{2,1,0:T(8,128)(2,1)} async-done(((bf16[16,1024,256]{2,1,0:T(8,128)(2,1)}), bf16[16,1024,256]{2,1,0:T(8,128)(2,1)}, u32[]{:S(2)}, u32[]{:S(2)}) %all-to-all-start) | async-done | bytes 8388640 | tf_op jit(solution)/shard_map/all_to_all | solution.py:44
  242.4 10.0 %multiply_reduce_fusion = f32[1024,256]{1,0:T(8,128)} fusion(f32[16,1024,256]{2,1,0:T(8,128)} %mul.61, bf16[16,1024,256]{2,1,0:T(8,128)(2,1)} %all-to-all-done), kind=kLoop, calls=%fused_computation.9 | loop fusion | flops 12320768 | bytes 26214400 | tf_op jit(solution)/shard_map/reduce_sum | solution.py:49
  252.5 363.0 %all-reduce.3.cloned.1.call-done = f32[16384]{0:T(1024)} async-done(((f32[16384]{0:T(1024)}), f32[16384]{0:T(1024)}) %all-reduce.3.cloned.1.call-update) | async-done | bytes 65552
  615.6 1.3 dynamic-slice
  (83 shorter events, 32.5 us)
Async XLA Ops:
  8.0 17.7 %copy-start.1 = (s32[1,1,2,16384]{3,2,1,0:T(2,128)S(1)}, s32[1,1,2,16384]{3,2,1,0:T(2,128)}, u32[]{:S(2)}) copy-start(s32[1,1,2,16384]{3,2,1,0:T(2,128)} %param.11) | copy-start | bytes 393220
  8.0 17.8 %copy-start = (bf16[128,256]{1,0:T(8,128)(2,1)S(1)}, bf16[128,256]{1,0:T(8,128)(2,1)}, u32[]{:S(2)}) copy-start(bf16[128,256]{1,0:T(8,128)(2,1)} %param.8) | copy-start | bytes 196612
  8.0 152.2 %all-gather.2.cloned.1.call-start = ((), (), s32[]{:S(2)}) async-start(), calls=%async_computation.4 | async-start | bytes 8912896 | tf_op jit(solution)/shard_map/all_gather | solution.py:52
  10.5 92.4 %all-to-all-start.1 = ((bf16[16,2,1024]{2,1,0:T(2,128)(2,1)}), bf16[16,2,1024]{2,1,0:T(2,128)(2,1)S(1)}, u32[]{:S(2)}, u32[]{:S(2)}) async-start(bf16[16,2,1024]{2,1,0:T(2,128)(2,1)} %copy.15), calls=%async_computation.1 | async-start | bytes 131072 | tf_op jit(solution)/shard_map/all_to_all | solution.py:45
  102.9 139.6 %all-to-all-start = ((bf16[16,1024,256]{2,1,0:T(8,128)(2,1)}), bf16[16,1024,256]{2,1,0:T(8,128)(2,1)}, u32[]{:S(2)}, u32[]{:S(2)}) async-start(bf16[16,1024,256]{2,1,0:T(8,128)(2,1)} %get-tuple-element.34), calls=%async_computation | async-start | bytes 16777216 | tf_op jit(solution)/shard_map/all_to_all | solution.py:44
  110.1 505.4 %all-reduce.3.cloned.1.call-start = ((), (), s32[]{:S(2)}) async-start(), calls=%async_computation.5 | async-start | bytes 131072
  168.3 448.5 %reduce-scatter.2.cloned.1.call-start = ((), (), s32[]{:S(2)}) async-start(), calls=%async_computation.3 | async-start | bytes 1081344 | tf_op jit(solution)/shard_map/reduce_scatter | solution.py:59
Sparse Core Ops, SparseCore 0:
  12.6 91.5 all-gather.1
  168.4 447.0 all-reduce.2
Sparse Core Ops, SparseCore 1:
  252.6 139.7 reduce-scatter.1
where the time goes:
time: 627 us; the launch traced here: 624 us
  waiting for transfers between devices  438 us (70%)
  local copies, waits for them, and re-layouts  84.6 us (13%)
  matrix products  41.6 us (7%)
  other arithmetic  20.2 us (3%)
  between operations  15.6 us (2%)
  starting transfers between devices  13.5 us (2%)
  loops' own time  10.9 us (2%)
    unnamed x4, waiting for transfers between devices  364 us
    all_to_all x1, waiting for transfers between devices, body(): lax.all_to_all(quantized, 'node', split_axis=0, concat_axis=0, tiled=True)  74.1 us
    mul x2, local copies, waits for them, and re-layouts, body(): restored * arrived_scales.astype(jnp.float32).transpose(0, 2, 1)[:, :, :,...  45.3 us
    dot_general x16, matrix products, quantize(): lax.dot_general(feature_cols, cotangent, (((0,), (0,)), ((), ())), prefer...  33.5 us
    mul x16, local copies, waits for them, and re-layouts, quantize(): partial_value.reshape(slab, block_count, block_width) * factor.T[:, :, None]  19.7 us
  transfers between devices with their start and end apart: 5, of which 2 were waited for; matrix products, arithmetic and copies ran while one was open for 23% of the time, Pallas kernels for 0%

commit v1 on v0

v1 whole, which is shorter than its diff:
```python
import functools

import jax
import jax.numpy as jnp
from jax import lax
from jax.experimental import pallas as pl
from jax.experimental.pallas import tpu as pltpu
from jax.sharding import PartitionSpec as P

EPSILON = 1e-05
SATURATE = 448.0
MESH = pl.DeviceIdType.MESH
F32 = jnp.float32
BF16 = jnp.bfloat16


def device(x, y, z, core):
    return ((x * 2 + lax.div(y, 2)) * 2 + core, z * 2 + lax.rem(y, 2))


def kernel(
    width, slab, nz,
    tok_hbm, cot_hbm, w_hbm, gain_hbm, exp_hbm,
    gw_ref, gg_ref,
    tokv, cotv, wv, gainv, expv, sibexp, invb, wall,
    usend, uown, urecv,
    p1, relp1, relm1, inm1, inp1,
    p2, relp2, relm2, inm2, inp2,
    hbuf, hx, hcross, hsum, zsrc, zrecv, fin, outt, hrow,
    loc_sem, tok_sem, core_s, core_r, exp_s, exp_r,
    agx_s, agx_r, agf_s, agf_r, agc_s, agc_r, ags_s, ags_r,
    st1_s, st1_r, st2_s, st2_r, hx_s, hx_r, hc_s, hc_r, z_s, z_r, fin_s, fin_r,
):
    node, rep = lax.axis_index("node"), lax.axis_index("rep")
    core = lax.rem(node, 2)
    yh = lax.rem(lax.div(node, 2), 2)
    x = lax.div(node, 4)
    yl = lax.rem(rep, 2)
    z = lax.div(rep, 2)
    y = yh * 2 + yl
    zl, zh = lax.rem(z, 2), lax.div(z, 2)
    zpair = z + 1 - 2 * zl
    ysame = yh * 2 + 1 - yl
    ycross = (1 - yh) * 2 + 1 - yl
    xs = [lax.rem(x + d, 4) for d in range(4)]
    ys = [lax.rem(y + d, 4) for d in range(4)]
    sibling = device(x, y, z, 1 - core)
    tiles = slab // 128

    def remote(src, dst, send, recv, where):
        return pltpu.make_async_remote_copy(
            src_ref=src, dst_ref=dst, send_sem=send, recv_sem=recv, device_id=where, device_id_type=MESH
        )

    loads = [
        pltpu.make_async_copy(w_hbm, wv, loc_sem.at[0]),
        pltpu.make_async_copy(cot_hbm, cotv, loc_sem.at[1]),
        pltpu.make_async_copy(gain_hbm, gainv, loc_sem.at[2]),
        pltpu.make_async_copy(exp_hbm, expv, loc_sem.at[3]),
    ]
    for load in loads:
        load.start()

    def token_load(s):
        at = pl.multiple_of(s * slab, slab)
        return pltpu.make_async_copy(tok_hbm.at[:, pl.ds(at, slab)], tokv.at[s], tok_sem.at[s])

    @pl.loop(0, 16)
    def _(s):
        token_load(s).start()

    barrier = pltpu.get_barrier_semaphore()
    partners = [
        sibling,
        device(xs[1], y, z, core), device(xs[2], y, z, core), device(xs[3], y, z, core),
        device(x, ys[1], z, core), device(x, ys[3], z, core),
        device(x, ysame, zpair, core),
    ]
    for where in partners:
        pl.semaphore_signal(barrier, inc=1, device_id=where, device_id_type=MESH)

    @pl.loop(1, nz)
    def _(d):
        pl.semaphore_signal(
            barrier, inc=1, device_id=device(x, y, lax.rem(z + d, nz), core), device_id_type=MESH
        )

    loads[0].wait()
    for t in range(tiles):
        for h in range(2):
            block = wv[t * 128 : (t + 1) * 128, h * 128 : (h + 1) * 128].astype(F32)
            wall[x, yh, h * 8 : (h + 1) * 8, :, t * 128 : (t + 1) * 128] = (
                block.T.astype(BF16).reshape(8, 16, 128)
            )
    loads[1].wait()
    loads[2].wait()
    loads[3].wait()
    pl.semaphore_wait(barrier, len(partners) + nz - 1)

    xplus, xminus = device(xs[1], y, z, core), device(xs[3], y, z, core)
    yplus, yminus = device(x, ys[1], z, core), device(x, ys[3], z, core)
    cross, same = device(x, ycross, z, core), device(x, ysame, z, core)
    half = pl.ds(0, 8), pl.ds(8, 8)
    hy = lax.rem(yh + yl, 2) * 8
    yhalf = pl.ds(hy, 8)

    def agx(k):
        return remote(wall.at[x, yh], wall.at[x, yh], agx_s.at[k], agx_r.at[k], (xplus, xminus)[k])

    def agf(k):
        ref = wall.at[xs[3 if k == 0 else 1], yh, half[k]]
        return remote(ref, ref, agf_s.at[k], agf_r.at[k], (xplus, xminus)[k])

    def agc(d):
        ref = wall.at[xs[d], yh, yhalf]
        return remote(ref, ref, agc_s.at[d], agc_r.at[d], cross)

    def ags(d):
        ref = wall.at[xs[d], 1 - yh, yhalf]
        return remote(ref, ref, ags_s.at[d], ags_r.at[d], same)

    agx(0).start()
    agx(1).start()
    agc(0).start()
    exps = remote(expv, sibexp, exp_s, exp_r, sibling)
    exps.start()

    def square(s, total):
        token_load(s).wait()
        for t in range(tiles):
            v = tokv[s, :, t * 128 : (t + 1) * 128].astype(F32)
            total = total + v * v
        return total

    total = lax.fori_loop(0, 16, square, jnp.zeros((128, 128), F32))
    inverse = lax.rsqrt(jnp.sum(total, axis=1, keepdims=True) * (1.0 / width) + EPSILON)
    step = min(slab, 256)
    invb[...] = jnp.broadcast_to(inverse, (128, step))
    cot_t = cotv[...].astype(F32).T.astype(BF16)

    def partial_slab(i, parity, out):
        s = i * 2 + parity
        for t in range(slab // step):
            g = gainv[:, pl.ds(pl.multiple_of(s * slab + t * step, step), step)].astype(F32)
            v = tokv[s, :, t * step : (t + 1) * step].astype(F32)
            normed = (v * invb[...] * g).astype(BF16)
            part = jnp.dot(cot_t, normed, preferred_element_type=F32)
            out[i, :, :, t * step : (t + 1) * step] = part.astype(BF16).reshape(16, 16, step)

    def core_copy(i):
        return remote(usend.at[i], urecv.at[i], core_s.at[i], core_r.at[i], sibling)

    @pl.loop(0, 8)
    def _(i):
        partial_slab(i, 1 - core, usend)
        core_copy(i).start()

    @pl.loop(0, 8)
    def _(i):
        partial_slab(i, core, uown)

    agx(0).wait_recv()
    agf(0).start()
    agc(3).start()
    agx(1).wait_recv()
    agf(1).start()
    agc(1).start()
    agc(0).wait_recv()
    ags(0).start()

    exps.wait_recv()
    parity_at = core * slab

    def threshold(ref, k, i):
        at = pl.multiple_of(i * 2 * slab + parity_at, slab)
        e = ref[k : k + 1, pl.ds(at, slab)]
        return jnp.left_shift(jnp.ones_like(e), e + 30).astype(F32) * (SATURATE * 2.0**-30)

    @pl.loop(0, 8)
    def _(i):
        core_copy(i).wait_recv()
        px, pyh = lax.div(i, 2), lax.rem(i, 2)
        for k in range(2):
            mine, theirs = threshold(expv, k, i), threshold(sibexp, k, i)
            for g in range(k * 8, k * 8 + 8):
                a = uown[i, g].astype(F32)
                b = urecv[i, g].astype(F32)
                a = jnp.minimum(jnp.maximum(a, -mine), mine)
                b = jnp.minimum(jnp.maximum(b, -theirs), theirs)
                q, lg = g // 4, g % 4
                value = (a + b).astype(BF16)
                if q % 2 == 0:
                    p1[q, px, lg // 2, pyh * 2 + lg % 2] = value
                else:
                    p1[q, pyh * 2 + lg // 2, lg % 2, px] = value

    def ring(q, stage):
        along_x = (q + stage) % 2 == 0
        plus, minus = (xplus, xminus) if along_x else (yplus, yminus)
        at = xs if along_x else ys
        p, relp, relm, inm, inp, ss, rs = (
            (p1, relp1, relm1, inm1, inp1, st1_s, st1_r),
            (p2, relp2, relm2, inm2, inp2, st2_s, st2_r),
        )[stage]

        def sem(k):
            return ss.at[q * 6 + k], rs.at[q * 6 + k]

        def copy(k):
            src, dst, where = (
                (p.at[q, at[2], 0], relp.at[q], plus),
                (p.at[q, at[2], 1], relm.at[q], minus),
                (p.at[q, at[1], 1], inm.at[q, 1], plus),
                (p.at[q, at[3], 0], inp.at[q, 0], minus),
                (p.at[q, at[1], 0], inm.at[q, 0], plus),
                (p.at[q, at[3], 1], inp.at[q, 1], minus),
            )[k]
            return remote(src, dst, *sem(k), where)

        return copy, at, p, relp, relm

    def ring_open(q, stage):
        copy = ring(q, stage)[0]
        for k in range(4):
            copy(k).start()

    def ring_relay(q, stage):
        copy, at, p, relp, relm = ring(q, stage)
        for c, d, h, rel in ((0, 1, 0, relp), (1, 3, 1, relm)):
            copy(c).wait_recv()
            if stage == 0:
                for m in range(4):
                    p[q, at[d], h, m] = (p[q, at[d], h, m].astype(F32) + rel[q, m].astype(F32)).astype(BF16)
            else:
                p[q, at[d], h] = (p[q, at[d], h].astype(F32) + rel[q].astype(F32)).astype(BF16)
            copy(4 + c).start()

    def ring_wait(q, stage):
        copy = ring(q, stage)[0]
        for k in range(2, 6):
            copy(k).wait_recv()

    for q in range(4):
        ring_open(q, 0)

    agf(0).wait_recv()
    agf(1).wait_recv()
    agc(2).start()
    agc(3).wait_recv()
    ags(3).start()
    agc(1).wait_recv()
    ags(1).start()

    for q in range(4):
        ring_relay(q, 0)

    agc(2).wait_recv()
    ags(2).start()
    for d in range(4):
        ags(d).wait_recv()

    @pl.loop(0, 8)
    def _(i):
        px, pyh = lax.div(i, 2), lax.rem(i, 2)
        total = jnp.zeros((16, slab), F32)
        for g in range(16):
            u = uown[i, g].astype(F32) + urecv[i, g].astype(F32)
            total = total + u * wall[px, pyh, g].astype(F32)
        at = pl.multiple_of(i * 2 * slab + parity_at, slab)
        row = jnp.sum(total, axis=0, keepdims=True) / gainv[:, pl.ds(at, slab)].astype(F32)
        if tiles < 8:
            hbuf[px, pyh] = jnp.zeros((8, 128), F32)
        for t in range(tiles):
            hbuf[px, pyh, t : t + 1, :] = row[:, t * 128 : (t + 1) * 128]

    def hx_copy(d):
        return remote(
            hbuf.at[xs[d]], hx.at[d], hx_s.at[d], hx_r.at[d], device(xs[d], y, z, core)
        )

    for d in range(1, 4):
        hx_copy(d).start()

    for q in range(4):
        ring_wait(q, 0)
        own = xs[0] if q % 2 == 0 else ys[0]
        for h in range(2):
            for m in range(4):
                value = (
                    p1[q, own, h, m].astype(F32) + inm1[q, h, m].astype(F32) + inp1[q, h, m].astype(F32)
                ).astype(BF16)
                if q % 2 == 0:
                    p2[q, (m // 2) * 2 + h, m % 2] = value
                else:
                    p2[q, m, h] = value
        ring_open(q, 1)

    for d in range(1, 4):
        hx_copy(d).wait_recv()
    hx[0] = hbuf[x] + hx[1] + hx[2] + hx[3]
    hc_copy = remote(hx.at[0, 1 - yh], hcross, hc_s, hc_r, cross)
    hc_copy.start()

    for q in range(4):
        ring_relay(q, 1)

    hc_copy.wait_recv()
    h_value = hx[0, yh] + hcross[...]
    hi = h_value.astype(BF16).astype(F32)
    hsum[0:8] = hi
    hsum[8:16] = h_value - hi
    split = hsum[...].astype(BF16)
    for zp in range(nz):
        zsrc[zp, 4] = split

    for q in range(4):
        ring_wait(q, 1)
        own = xs[0] if q % 2 == 1 else ys[0]
        for h in range(2):
            value = (
                p2[q, own, h].astype(F32) + inm2[q, h].astype(F32) + inp2[q, h].astype(F32)
            ).astype(BF16)
            for t in range(tiles):
                zsrc[t * 2 + h, q] = value[:, t * 128 : (t + 1) * 128]

    def z_copy(d):
        there = lax.rem(z + d, nz)
        return remote(zsrc.at[there], zrecv.at[d], z_s.at[d], z_r.at[d], device(x, y, there, core))

    @pl.loop(1, nz)
    def _(d):
        z_copy(d).start()

    mine = yl * 2 + zl
    fin[mine] = zsrc[z].astype(F32)

    @pl.loop(1, nz)
    def _(d):
        z_copy(d).wait_recv()
        fin[mine] += zrecv[d].astype(F32)

    ends = [device(x, y, zpair, core), device(x, ysame, z, core), device(x, ysame, zpair, core)]
    fin_copies = [
        remote(fin.at[mine], fin.at[mine], fin_s.at[k], fin_r.at[k], ends[k]) for k in range(3)
    ]
    for copy in fin_copies:
        copy.start()

    for k in range(2):
        agx(k).wait_send()
        agf(k).wait_send()
    for d in range(4):
        agc(d).wait_send()
        ags(d).wait_send()
    exps.wait_send()

    @pl.loop(0, 8)
    def _(i):
        core_copy(i).wait_send()

    for stage in range(2):
        for q in range(4):
            copy = ring(q, stage)[0]
            for k in range(6):
                copy(k).wait_send()
    for d in range(1, 4):
        hx_copy(d).wait_send()
    hc_copy.wait_send()

    @pl.loop(1, nz)
    def _(d):
        z_copy(d).wait_send()

    for copy in fin_copies:
        copy.wait()
    place = zl * 2 + yl
    for q in range(4):
        block = fin[:, q].reshape(64, 128)
        outt[:, q * 64 : (q + 1) * 64] = block.T
    gw_ref[...] = outt[pl.ds(pl.multiple_of(place * 32, 32), 32), :]
    both = fin[mine, 4] + fin[(1 - yl) * 2 + zl, 4]
    h_all = both[0:8] + both[8:16]
    hrow[...] = pltpu.roll(h_all, lax.rem(128 - place * 32, 128), 1)
    gg_ref[...] = hrow[pl.ds(zh, 1), 0:32]


def body(tokens, cotangent, weight, gain, exponents):
    width = tokens.shape[1]
    nz = lax.axis_size("rep") // 2
    slab = width // 16
    dma = pltpu.SemaphoreType.DMA
    vmem = pltpu.VMEM
    scratch = [
        vmem((16, 128, slab), BF16),
        vmem((128, 256), BF16),
        vmem((slab, 256), BF16),
        vmem((1, width), BF16),
        vmem((2, width), jnp.int32),
        vmem((2, width), jnp.int32),
        vmem((128, min(slab, 256)), F32),
        vmem((4, 2, 16, 16, slab), BF16),
        vmem((8, 16, 16, slab), BF16),
        vmem((8, 16, 16, slab), BF16),
        vmem((8, 16, 16, slab), BF16),
        vmem((4, 4, 2, 4, 16, slab), BF16),
        vmem((4, 4, 16, slab), BF16),
        vmem((4, 4, 16, slab), BF16),
        vmem((4, 2, 4, 16, slab), BF16),
        vmem((4, 2, 4, 16, slab), BF16),
        vmem((4, 4, 2, 16, slab), BF16),
        vmem((4, 16, slab), BF16),
        vmem((4, 16, slab), BF16),
        vmem((4, 2, 16, slab), BF16),
        vmem((4, 2, 16, slab), BF16),
        vmem((4, 2, 8, 128), F32),
        vmem((4, 2, 8, 128), F32),
        vmem((8, 128), F32),
        vmem((16, 128), F32),
        vmem((nz, 5, 16, 128), BF16),
        vmem((nz, 5, 16, 128), BF16),
        vmem((4, 5, 16, 128), F32),
        vmem((128, 256), F32),
        vmem((8, 128), F32),
        dma((4,)), dma((16,)), dma((8,)), dma((8,)), dma, dma,
        dma((2,)), dma((2,)), dma((2,)), dma((2,)), dma((4,)), dma((4,)), dma((4,)), dma((4,)),
        dma((24,)), dma((24,)), dma((24,)), dma((24,)), dma((4,)), dma((4,)), dma, dma,
        dma((nz,)), dma((nz,)), dma((3,)), dma((3,)),
    ]
    any_space = pl.BlockSpec(memory_space=pl.ANY)
    grad_weight, grad_gain = pl.pallas_call(
        functools.partial(kernel, width, slab, nz),
        out_shape=(
            jax.ShapeDtypeStruct((32, 256), F32),
            jax.ShapeDtypeStruct((1, 32), F32),
        ),
        in_specs=[any_space] * 5,
        out_specs=(pl.BlockSpec(memory_space=pltpu.VMEM),) * 2,
        scratch_shapes=scratch,
        compiler_params=pltpu.CompilerParams(
            collective_id=0, has_side_effects=True, vmem_limit_bytes=48 * 2**20
        ),
    )(tokens, cotangent, weight, gain.reshape(1, width), exponents.reshape(2, width))
    return (grad_weight, grad_gain.reshape(32))


def solution(mesh):
    placed = (
        P(("node", "rep"), None),
        P(("node", "rep"), None),
        P("node", None),
        P(),
        P("node", "rep", None, None),
    )
    return jax.shard_map(
        body,
        mesh=mesh,
        in_specs=placed,
        out_specs=(P(("node", "rep"), None), P(("node", "rep"))),
        check_vma=False,
    )
```

time: 627 us -> 109 us (0.17)
  waiting for transfers between devices: 438 us -> 0 us
  Pallas kernels: 0 us -> 101 us
  local copies, waits for them, and re-layouts: 84.6 us -> 6.89 us
  matrix products: 41.6 us -> 0 us
  other arithmetic: 20.2 us -> 0 us
  between operations: 15.6 us -> 0.65 us
  starting transfers between devices: 13.5 us -> 0 us
  loops' own time: 10.9 us -> 0 us
    unnamed x4 -> x0, waiting for transfers between devices: 364 us -> none
    pallas_call x0 -> x1, Pallas kernels: none -> 101 us  [body(): pl.pallas_call(functools.partial(kernel, width, slab, nz), out_shape=(jax...]
    all_to_all x2 -> x0, waiting for transfers between devices: 74.1 us -> none  [the longest x1 74.1 us: body(): lax.all_to_all(quantized, 'node', split_axis=0, concat_axis=0, tiled=True)]
    mul x18 -> x0, local copies, waits for them, and re-layouts: 65 us -> none  [the longest x2 45.3 us: body(): restored * arrived_scales.astype(jnp.float32).transpose(0, 2, 1)[:, :, :,...]
    dot_general x17 -> x0, matrix products: 41.6 us -> none  [the longest x16 33.5 us: quantize(): lax.dot_general(feature_cols, cotangent, (((0,), (0,)), ((), ())), prefer...]
    all_to_all x2 -> x0, starting transfers between devices: 13.4 us -> none  [the longest x1 7.26 us: body(): lax.all_to_all(quantized, 'node', split_axis=0, concat_axis=0, tiled=True)]
    reduce_sum x2 -> x0, other arithmetic: 13.1 us -> none  [the longest x1 10 us: body(): node_total = jnp.sum(restored, axis=0).reshape(slab, kv_width)]
    dynamic_slice x48 -> x0, local copies, waits for them, and re-layouts: 13 us -> none  [the longest x16 9.32 us: body(): quantized = lax.map(quantize, jnp.arange(node_count, dtype=jnp.int32))]
  transfers between devices with their start and end apart: 5 -> 0, of which waited for: 2 -> 0; matrix products, arithmetic and copies ran while one was open for 23% -> 0% of each run, Pallas kernels for 0% -> 0%
where the time goes in v1:
time: 109 us; the launch traced here: 108 us
  Pallas kernels  101 us (93%)
  local copies, waits for them, and re-layouts  6.89 us (6%)
    pallas_call x1, Pallas kernels, body(): pl.pallas_call(functools.partial(kernel, width, slab, nz), out_shape=(jax...  101 us
    unnamed x10, local copies, waits for them, and re-layouts  6.1 us

profile of v1, /device:TPU:8, one launch (start us, length us, event | category | flops | bytes accessed | tf_op | source)
XLA Modules:
  0.0 108.4 jit_solution(5108074048065427627)
XLA Ops:
  0.6 0.8 reshape.13.gain_hbm
  1.4 0.0 copy-start
  1.4 2.2 %copy-done = bf16[128,16384]{1,0:T(8,128)(2,1)S(1)} copy-done((bf16[128,16384]{1,0:T(8,128)(2,1)S(1)}, bf16[128,16384]{1,0:T(8,128)(2,1)}, u32[]{:S(2)}) %copy-start) | copy-done | bytes 4194328
  3.6 0.0 copy-start.1
  3.6 1.0 copy-done.1
  4.7 0.0 copy-start.2
  4.7 0.9 copy-done.2
  5.6 0.0 copy-start.3
  5.6 0.8 copy-done.3
  6.4 100.8 %shard_map.68 = (f32[32,256]{1,0:T(8,128)S(1)}, f32[1,32]{1,0:T(1,128)S(1)}) custom-call(bf16[128,16384]{1,0:T(8,128)(2,1)S(1)} %copy-done, bf16[128,256]{1,0:T(8,128)(2,1)S(1)} %copy-done.3, bf16[1024,256]{1,0:T(8,128)(2,1)S(1)} %copy-done.1, bf16[1,16384]{1,0:T(2,128)(2,1)S(1)} %reshape.13.gain_hbm, s32[2,16384]{1,0:T(2,128)S(1)} %bitcast.2), custom_call_target="tpu_custom_call" | custom-call | tf_op jit(solution)/shard_map/pallas_call | solution.py:430
  107.2 0.6 copy.9
  107.9 0.5 copy.10
Async XLA Ops:
  1.4 2.2 %copy-start = (bf16[128,16384]{1,0:T(8,128)(2,1)S(1)}, bf16[128,16384]{1,0:T(8,128)(2,1)}, u32[]{:S(2)}) copy-start(bf16[128,16384]{1,0:T(8,128)(2,1)} %tok_hbm.1) | copy-start | bytes 12582916
  3.6 1.0 copy-start.1
  4.7 0.9 copy-start.2
  5.6 0.8 copy-start.3

commit v2 on v1

v2 whole, which is shorter than its diff:
```python
import functools

import jax
import jax.numpy as jnp
from jax import lax
from jax.experimental import pallas as pl
from jax.experimental.pallas import tpu as pltpu
from jax.sharding import PartitionSpec as P

EPSILON = 1e-05
SATURATE = 448.0
MESH = pl.DeviceIdType.MESH
F32 = jnp.float32
BF16 = jnp.bfloat16


def device(x, y, z, core):
    return ((x * 2 + lax.div(y, 2)) * 2 + core, z * 2 + lax.rem(y, 2))


def kernel(
    width, slab, nz,
    tok_hbm, cot_hbm, w_hbm, gain_hbm, exp_hbm,
    gw_ref, gg_ref,
    tokv, cotv, wv, gainv, expv, sibexp, invb, wall,
    usend, uown, urecv,
    p1, relp1, relm1, inm1, inp1,
    p2, in2,
    hbuf, hx, hcross, zsrc0, zsrc1, zrecv0, zrecv1, zhsrc, zhrecv, fin, outt, hrow,
    heard, loc_sem, tok_sem, core_s, core_r, exp_s, exp_r,
    agx_s, agx_r, agf_s, agf_r, agc_s, agc_r, ags_s, ags_r, agz_s, agz_r,
    st1_s, st1_r, st2_s, st2_r, hx_s, hx_r, hc_s, hc_r, z_s, z_r, zh_s, zh_r, fin_s, fin_r,
):
    node, rep = lax.axis_index("node"), lax.axis_index("rep")
    core = lax.rem(node, 2)
    yh = lax.rem(lax.div(node, 2), 2)
    x = lax.div(node, 4)
    yl = lax.rem(rep, 2)
    z = lax.div(rep, 2)
    y = yh * 2 + yl
    zl, zh = lax.rem(z, 2), lax.div(z, 2)
    zpair = z + 1 - 2 * zl
    ysame = yh * 2 + 1 - yl
    ycross = (1 - yh) * 2 + 1 - yl
    xs = [lax.rem(x + d, 4) for d in range(4)]
    ys = [lax.rem(y + d, 4) for d in range(4)]
    sibling = device(x, y, z, 1 - core)
    tiles = slab // 128

    def remote(src, dst, send, recv, where):
        return pltpu.make_async_remote_copy(
            src_ref=src, dst_ref=dst, send_sem=send, recv_sem=recv, device_id=where, device_id_type=MESH
        )

    loads = [
        pltpu.make_async_copy(w_hbm, wv, loc_sem.at[0]),
        pltpu.make_async_copy(cot_hbm, cotv, loc_sem.at[1]),
        pltpu.make_async_copy(gain_hbm, gainv, loc_sem.at[2]),
        pltpu.make_async_copy(exp_hbm, expv, loc_sem.at[3]),
    ]
    for load in loads:
        load.start()

    def token_load(s):
        at = pl.multiple_of(s * slab, slab)
        return pltpu.make_async_copy(tok_hbm.at[:, pl.ds(at, slab)], tokv.at[s], tok_sem.at[s])

    @pl.loop(0, 16)
    def _(s):
        token_load(s).start()

    barrier = pltpu.get_barrier_semaphore()
    zplus, zminus = lax.rem(z + 1, nz), lax.rem(z + nz - 1, nz)
    partners = [
        sibling,
        device(xs[1], y, z, core), device(xs[2], y, z, core), device(xs[3], y, z, core),
        device(x, ys[1], z, core), device(x, ys[2], z, core), device(x, ys[3], z, core),
        device(x, y, zplus, core), device(x, y, zminus, core),
    ]
    for where in partners:
        pl.semaphore_signal(barrier, inc=1, device_id=where, device_id_type=MESH)

    def tell(k):
        far = 2**k
        listeners = [device(x, y, lax.rem(z + far, nz), core), device(x, y, lax.rem(z + nz - far, nz), core)]
        if k == 0:
            listeners.append(device(x, ysame, z, core))
        if far == 1 or 2 * far < nz:
            for where in listeners:
                pl.semaphore_signal(heard.at[k], inc=1, device_id=where, device_id_type=MESH)

    def hear(k):
        if 2**k == 1 or 2 ** (k + 1) < nz:
            pl.semaphore_wait(heard.at[k], 3 if k == 0 else 2)

    loads[0].wait()
    for t in range(tiles):
        for h in range(2):
            block = wv[t * 128 : (t + 1) * 128, h * 128 : (h + 1) * 128].astype(F32)
            wall[x, yh, h * 8 : (h + 1) * 8, :, t * 128 : (t + 1) * 128] = (
                block.T.astype(BF16).reshape(8, 16, 128)
            )
    loads[1].wait()
    loads[2].wait()
    loads[3].wait()

    xplus, xminus = device(xs[1], y, z, core), device(xs[3], y, z, core)
    yplus, yminus = device(x, ys[1], z, core), device(x, ys[3], z, core)
    cross, same = device(x, ycross, z, core), device(x, ysame, z, core)
    hy = lax.rem(yh + yl, 2)
    first = zl * 8
    yquarter = pl.ds(first + hy * 4, 4)

    def agx(d, k):
        ref = wall.at[x, yh, pl.ds(first + 4 * k, 4)]
        n = d - 1 + k
        return remote(ref, ref, agx_s.at[n], agx_r.at[n], device(xs[d], y, z, core))

    def agf(k):
        ref = wall.at[xs[3 - 2 * k], yh, pl.ds(first + 4 * k, 4)]
        return remote(ref, ref, agf_s.at[k], agf_r.at[k], (xplus, xminus)[k])

    def agc(d):
        ref = wall.at[xs[d], yh, yquarter]
        return remote(ref, ref, agc_s.at[d], agc_r.at[d], cross)

    def ags(d):
        ref = wall.at[xs[d], 1 - yh, yquarter]
        return remote(ref, ref, ags_s.at[d], ags_r.at[d], same)

    def agz(k, d, e):
        ref = wall.at[xs[d], yh if e == 0 else 1 - yh, pl.ds(first + 4 * k, 4)]
        n = k * 8 + e * 4 + d
        there = device(x, y, lax.rem(z + nz + 2 * k - 1, nz), core)
        return remote(ref, ref, agz_s.at[n], agz_r.at[n], there)

    z_sends = [(k, d, e) for k in range(2) for d in range(4) for e in range(2) if d + e]

    def from_x(k):
        agx(1, k).wait_recv()
        agx(3, k).wait_recv()
        agf(k).start()
        agz(k, 3, 0).start()
        agz(k, 1, 0).start()

    def from_opposite():
        for k in range(2):
            agf(k).wait_recv()
            agz(k, 2, 0).start()
        agc(2).start()

    def from_cross(d):
        agc(d).wait_recv()
        ags(d).start()
        agz(hy, d, 1).start()

    def from_same(d):
        ags(d).wait_recv()
        agz(1 - hy, d, 1).start()

    def square(s, total):
        token_load(s).wait()
        for t in range(tiles):
            v = tokv[s, :, t * 128 : (t + 1) * 128].astype(F32)
            total = total + v * v
        return total

    total = lax.fori_loop(0, 16, square, jnp.zeros((128, 128), F32))
    inverse = lax.rsqrt(jnp.sum(total, axis=1, keepdims=True) * (1.0 / width) + EPSILON)
    step = min(slab, 256)
    invb[...] = jnp.broadcast_to(inverse, (128, step))
    cot_t = cotv[...].astype(F32).T.astype(BF16)

    def partial_slab(i, parity, out):
        s = i * 2 + parity
        for t in range(slab // step):
            g = gainv[:, pl.ds(pl.multiple_of(s * slab + t * step, step), step)].astype(F32)
            v = tokv[s, :, t * step : (t + 1) * step].astype(F32)
            normed = (v * invb[...] * g).astype(BF16)
            part = jnp.dot(cot_t, normed, preferred_element_type=F32)
            out[i, :, :, t * step : (t + 1) * step] = part.astype(BF16).reshape(16, 16, step)

    def core_copy(q):
        rows = pl.ds(4 * q, 4)
        return remote(usend.at[:, rows], urecv.at[:, rows], core_s.at[q], core_r.at[q], sibling)

    exps = remote(expv, sibexp, exp_s, exp_r, sibling)

    @pl.loop(0, 8)
    def _(i):
        partial_slab(i, 1 - core, usend)

    pl.semaphore_wait(barrier, len(partners))
    tell(0)
    exps.start()
    core_copy(0).start()
    agx(1, 0).start()
    agx(3, 0).start()
    agx(1, 1).start()
    agx(3, 1).start()
    agc(0).start()
    core_copy(1).start()
    core_copy(2).start()
    core_copy(3).start()

    @pl.loop(0, 8)
    def _(i):
        partial_slab(i, core, uown)

    hear(0)
    tell(1)

    exps.wait_recv()
    parity_at = core * slab

    def threshold(ref, k, i):
        at = pl.multiple_of(i * 2 * slab + parity_at, slab)
        e = ref[k : k + 1, pl.ds(at, slab)]
        return jnp.left_shift(jnp.ones_like(e), e + 30).astype(F32) * (SATURATE * 2.0**-30)

    def combine(q):
        k = q // 2
        core_copy(q).wait_recv()

        @pl.loop(0, 8)
        def _(i):
            px, pyh = lax.div(i, 2), lax.rem(i, 2)
            mine, theirs = threshold(expv, k, i), threshold(sibexp, k, i)
            for lg in range(4):
                a = uown[i, q * 4 + lg].astype(F32)
                b = urecv[i, q * 4 + lg].astype(F32)
                a = jnp.minimum(jnp.maximum(a, -mine), mine)
                b = jnp.minimum(jnp.maximum(b, -theirs), theirs)
                value = (a + b).astype(BF16)
                if q % 2 == 0:
                    p1[q, px, lg // 2, pyh * 2 + lg % 2] = value
                else:
                    p1[q, pyh * 2 + lg // 2, lg % 2, px] = value

    def ring(q, k):
        plus, minus = (xplus, xminus) if q % 2 == 0 else (yplus, yminus)
        at = xs if q % 2 == 0 else ys
        src, dst, where = (
            (p1.at[q, at[2], 0], relp1.at[q], plus),
            (p1.at[q, at[2], 1], relm1.at[q], minus),
            (p1.at[q, at[1], 1], inm1.at[q, 1], plus),
            (p1.at[q, at[3], 0], inp1.at[q, 0], minus),
            (p1.at[q, at[1], 0], inm1.at[q, 0], plus),
            (p1.at[q, at[3], 1], inp1.at[q, 1], minus),
        )[k]
        return remote(src, dst, st1_s.at[q * 6 + k], st1_r.at[q * 6 + k], where)

    def ring_open(q):
        for k in range(4):
            ring(q, k).start()

    def ring_relay(q):
        at = xs if q % 2 == 0 else ys
        for c, d, h, rel in ((0, 1, 0, relp1), (1, 3, 1, relm1)):
            ring(q, c).wait_recv()
            for m in range(4):
                p1[q, at[d], h, m] = (p1[q, at[d], h, m].astype(F32) + rel[q, m].astype(F32)).astype(BF16)
            ring(q, 4 + c).start()

    def direct(q, d):
        there = device(xs[d], y, z, core) if q % 2 == 1 else device(x, ys[d], z, core)
        at = xs if q % 2 == 1 else ys
        n = q * 4 + d
        return remote(p2.at[q, at[d]], in2.at[q, d], st2_s.at[n], st2_r.at[n], there)

    def ring_close(q):
        for k in range(2, 6):
            ring(q, k).wait_recv()
        own = xs[0] if q % 2 == 0 else ys[0]
        for h in range(2):
            for m in range(4):
                value = (
                    p1[q, own, h, m].astype(F32) + inm1[q, h, m].astype(F32) + inp1[q, h, m].astype(F32)
                ).astype(BF16)
                if q % 2 == 0:
                    p2[q, (m // 2) * 2 + h, m % 2] = value
                else:
                    p2[q, m, h] = value
        for d in (2, 1, 3):
            direct(q, d).start()

    def gain_terms():
        @pl.loop(0, 8)
        def _(i):
            px, pyh = lax.div(i, 2), lax.rem(i, 2)
            total = jnp.zeros((16, slab), F32)
            for g in range(16):
                u = uown[i, g].astype(F32) + urecv[i, g].astype(F32)
                total = total + u * wall[px, pyh, g].astype(F32)
            at = pl.multiple_of(i * 2 * slab + parity_at, slab)
            row = jnp.sum(total, axis=0, keepdims=True) / gainv[:, pl.ds(at, slab)].astype(F32)
            if tiles < 8:
                hbuf[px, pyh] = jnp.zeros((8, 128), F32)
            for t in range(tiles):
                hbuf[px, pyh, t : t + 1, :] = row[:, t * 128 : (t + 1) * 128]

    def hx_copy(d):
        return remote(
            hbuf.at[xs[d]], hx.at[d], hx_s.at[d], hx_r.at[d], device(xs[d], y, z, core)
        )

    def finish(q):
        own = xs[0] if q % 2 == 1 else ys[0]
        for d in (1, 2, 3):
            direct(q, d).wait_recv()
        zsrc = (zsrc0, zsrc1)[q // 2]
        for h in range(2):
            value = (
                p2[q, own, h].astype(F32)
                + in2[q, 1, h].astype(F32) + in2[q, 2, h].astype(F32) + in2[q, 3, h].astype(F32)
            ).astype(BF16)
            for t in range(tiles):
                zsrc[t * 2 + h, q % 2] = value[:, t * 128 : (t + 1) * 128]

    def z_copy(b, d):
        there = lax.rem(z + d, nz)
        src, dst = ((zsrc0, zrecv0), (zsrc1, zrecv1))[b]
        n = b * nz + d
        return remote(src.at[there], dst.at[d], z_s.at[n], z_r.at[n], device(x, y, there, core))

    def zh_copy(d):
        there = lax.rem(z + d, nz)
        return remote(zhsrc, zhrecv.at[d], zh_s.at[d], zh_r.at[d], device(x, y, there, core))

    def z_send(b):
        @pl.loop(1, nz)
        def _(d):
            z_copy(b, d).start()

    hc_copy = remote(hx.at[0, 1 - yh], hcross, hc_s, hc_r, cross)

    def gain_start():
        for k, d, e in z_sends:
            agz(k, d, e).wait_recv()
        gain_terms()
        for d in range(1, 4):
            hx_copy(d).start()

    def gain_cross():
        for d in range(1, 4):
            hx_copy(d).wait_recv()
        hx[0] = hbuf[x] + hx[1] + hx[2] + hx[3]
        hc_copy.start()

    def gain_z():
        hc_copy.wait_recv()
        zhsrc[...] = hx[0, yh] + hcross[...]

        @pl.loop(1, nz)
        def _(d):
            zh_copy(d).start()

    from_x(0)
    combine(0)
    ring_open(0)
    from_x(1)
    agc(3).start()
    agc(1).start()
    combine(1)
    ring_open(1)
    from_cross(0)
    combine(2)
    combine(3)
    hear(1)
    tell(2)
    ring_relay(0)
    ring_relay(1)
    from_opposite()
    ring_open(2)
    ring_open(3)
    for d in (3, 1):
        from_cross(d)
    from_same(0)
    ring_relay(2)
    ring_relay(3)
    from_cross(2)
    for d in (3, 1):
        from_same(d)
    ring_close(0)
    ring_close(1)
    from_same(2)
    hear(2)
    ring_close(2)
    ring_close(3)
    finish(0)
    finish(1)
    z_send(0)
    finish(2)
    finish(3)
    z_send(1)
    gain_start()
    gain_cross()
    gain_z()

    mine = yl * 2 + zl
    fin[mine, 0:2] = zsrc0[z].astype(F32)
    fin[mine, 2:4] = zsrc1[z].astype(F32)
    fin[mine, 4, 0:8] = zhsrc[...]
    fin[mine, 4, 8:16] = jnp.zeros((8, 128), F32)

    for b in range(2):

        @pl.loop(1, nz)
        def _(d):
            z_copy(b, d).wait_recv()
            if b == 0:
                fin[mine, 0:2] += zrecv0[d].astype(F32)
            else:
                fin[mine, 2:4] += zrecv1[d].astype(F32)

    @pl.loop(1, nz)
    def _(d):
        zh_copy(d).wait_recv()
        fin[mine, 4, 0:8] += zhrecv[d]

    ends = [device(x, y, zpair, core), device(x, ysame, z, core), device(x, ysame, zpair, core)]
    fin_copies = [
        remote(fin.at[mine], fin.at[mine], fin_s.at[k], fin_r.at[k], ends[k]) for k in range(3)
    ]
    for copy in fin_copies:
        copy.start()

    for d in range(1, 4):
        hx_copy(d).wait_send()
    for k in range(2):
        agx(1, k).wait_send()
        agx(3, k).wait_send()
        agf(k).wait_send()
    for d in range(4):
        agc(d).wait_send()
        ags(d).wait_send()
    for k, d, e in z_sends:
        agz(k, d, e).wait_send()
    exps.wait_send()
    hc_copy.wait_send()

    for q in range(4):
        core_copy(q).wait_send()
        for k in range(6):
            ring(q, k).wait_send()
        for d in range(1, 4):
            direct(q, d).wait_send()

    for b in range(2):

        @pl.loop(1, nz)
        def _(d):
            z_copy(b, d).wait_send()

    @pl.loop(1, nz)
    def _(d):
        zh_copy(d).wait_send()

    for copy in fin_copies:
        copy.wait()
    place = zl * 2 + yl
    for q in range(4):
        block = fin[:, q].reshape(64, 128)
        outt[:, q * 64 : (q + 1) * 64] = block.T
    gw_ref[...] = outt[pl.ds(pl.multiple_of(place * 32, 32), 32), :]
    both = fin[mine, 4] + fin[(1 - yl) * 2 + zl, 4]
    hrow[...] = pltpu.roll(both[0:8], lax.rem(128 - place * 32, 128), 1)
    gg_ref[...] = hrow[pl.ds(zh, 1), 0:32]


def body(tokens, cotangent, weight, gain, exponents):
    width = tokens.shape[1]
    nz = lax.axis_size("rep") // 2
    slab = width // 16
    dma = pltpu.SemaphoreType.DMA
    vmem = pltpu.VMEM
    scratch = [
        vmem((16, 128, slab), BF16),
        vmem((128, 256), BF16),
        vmem((slab, 256), BF16),
        vmem((1, width), BF16),
        vmem((2, width), jnp.int32),
        vmem((2, width), jnp.int32),
        vmem((128, min(slab, 256)), F32),
        vmem((4, 2, 16, 16, slab), BF16),
        vmem((8, 16, 16, slab), BF16),
        vmem((8, 16, 16, slab), BF16),
        vmem((8, 16, 16, slab), BF16),
        vmem((4, 4, 2, 4, 16, slab), BF16),
        vmem((4, 4, 16, slab), BF16),
        vmem((4, 4, 16, slab), BF16),
        vmem((4, 2, 4, 16, slab), BF16),
        vmem((4, 2, 4, 16, slab), BF16),
        vmem((4, 4, 2, 16, slab), BF16),
        vmem((4, 4, 2, 16, slab), BF16),
        vmem((4, 2, 8, 128), F32),
        vmem((4, 2, 8, 128), F32),
        vmem((8, 128), F32),
        vmem((nz, 2, 16, 128), BF16),
        vmem((nz, 2, 16, 128), BF16),
        vmem((nz, 2, 16, 128), BF16),
        vmem((nz, 2, 16, 128), BF16),
        vmem((8, 128), F32),
        vmem((nz, 8, 128), F32),
        vmem((4, 5, 16, 128), F32),
        vmem((128, 256), F32),
        vmem((8, 128), F32),
        pltpu.SemaphoreType.REGULAR((3,)),
        dma((4,)), dma((16,)), dma((4,)), dma((4,)), dma, dma,
        dma((4,)), dma((4,)), dma((2,)), dma((2,)), dma((4,)), dma((4,)), dma((4,)), dma((4,)),
        dma((16,)), dma((16,)),
        dma((24,)), dma((24,)), dma((16,)), dma((16,)), dma((4,)), dma((4,)), dma, dma,
        dma((2 * nz,)), dma((2 * nz,)), dma((nz,)), dma((nz,)), dma((3,)), dma((3,)),
    ]
    any_space = pl.BlockSpec(memory_space=pl.ANY)
    grad_weight, grad_gain = pl.pallas_call(
        functools.partial(kernel, width, slab, nz),
        out_shape=(
            jax.ShapeDtypeStruct((32, 256), F32),
            jax.ShapeDtypeStruct((1, 32), F32),
        ),
        in_specs=[any_space] * 5,
        out_specs=(pl.BlockSpec(memory_space=pltpu.VMEM),) * 2,
        scratch_shapes=scratch,
        compiler_params=pltpu.CompilerParams(
            collective_id=0, has_side_effects=True, vmem_limit_bytes=60 * 2**20
        ),
    )(tokens, cotangent, weight, gain.reshape(1, width), exponents.reshape(2, width))
    return (grad_weight, grad_gain.reshape(32))


def solution(mesh):
    placed = (
        P(("node", "rep"), None),
        P(("node", "rep"), None),
        P("node", None),
        P(),
        P("node", "rep", None, None),
    )
    return jax.shard_map(
        body,
        mesh=mesh,
        in_specs=placed,
        out_specs=(P(("node", "rep"), None), P(("node", "rep"))),
        check_vma=False,
    )
```

time: 109 us -> 91.5 us (0.84)
  the two profiles are of different devices: /device:TPU:8 before, /device:TPU:64 now
where the time goes in v2:
time: 91.5 us; the launch traced here: 91.3 us
  Pallas kernels  86.6 us (95%)
  local copies, waits for them, and re-layouts  3.98 us (4%)
    pallas_call x1, Pallas kernels, body(): pl.pallas_call(functools.partial(kernel, width, slab, nz), out_shape=(jax...  86.6 us
    unnamed x2, local copies, waits for them, and re-layouts  2.57 us

profile of v2, /device:TPU:64, one launch (start us, length us, event | category | flops | bytes accessed | tf_op | source)
XLA Modules:
  0.0 91.3 jit_solution(12769485162451691761)
XLA Ops:
  0.6 1.4 %reshape.13.gain_hbm = bf16[1,16384]{1,0:T(2,128)(2,1)} reshape(bf16[16384]{0:T(1024)(128)(2,1)} %param.8) | data formatting | bytes 65536 | tf_op jit(solution)/shard_map/reshape | solution.py:528
  2.0 86.6 %shard_map.68 = (f32[32,256]{1,0:T(8,128)}, f32[1,32]{1,0:T(1,128)}) custom-call(bf16[128,16384]{1,0:T(8,128)(2,1)} %tok_hbm.1, bf16[128,256]{1,0:T(8,128)(2,1)} %cot_hbm.1, bf16[1024,256]{1,0:T(8,128)(2,1)} %w_hbm.1, bf16[1,16384]{1,0:T(2,128)(2,1)} %reshape.13.gain_hbm, s32[2,16384]{1,0:T(2,128)} %bitcast.2), custom_call_target="tpu_custom_call" | custom-call | tf_op jit(solution)/shard_map/pallas_call | solution.py:516
  88.7 1.4 %copy.9 = f32[32,256]{1,0:T(8,128)} copy(f32[32,256]{1,0:T(8,128)} %get-tuple-element.8) | data formatting | bytes 65536
  90.1 1.2 %copy.10 = f32[32]{0:T(128)} copy(f32[32]{0:T(128)} %bitcast.3) | data formatting | bytes 256

commit v3 on v2

--- a/solution.py
+++ b/solution.py
@@ -26,10 +26,10 @@
     usend, uown, urecv,
     p1, relp1, relm1, inm1, inp1,
     p2, in2,
-    hbuf, hx, hcross, zsrc0, zsrc1, zrecv0, zrecv1, zhsrc, zhrecv, fin, outt, hrow,
+    hbuf, hx, hcross, hpair, zxsrc, zxrecv, zown, zsrc0, zsrc1, zrecv0, zrecv1, zhsrc, zhrecv, fin, outt,
     heard, loc_sem, tok_sem, core_s, core_r, exp_s, exp_r,
     agx_s, agx_r, agf_s, agf_r, agc_s, agc_r, ags_s, ags_r, agz_s, agz_r,
-    st1_s, st1_r, st2_s, st2_r, hx_s, hx_r, hc_s, hc_r, z_s, z_r, zh_s, zh_r, fin_s, fin_r,
+    st1_s, st1_r, st2_s, st2_r, hx_s, hx_r, hc_s, hc_r, hz_s, hz_r, zx_s, zx_r, z_s, z_r, zh_s, zh_r, fin_s, fin_r,
 ):
     node, rep = lax.axis_index("node"), lax.axis_index("rep")
     core = lax.rem(node, 2)
@@ -304,31 +304,47 @@
             hbuf.at[xs[d]], hx.at[d], hx_s.at[d], hx_r.at[d], device(xs[d], y, z, core)
         )
 
+    def pair_copy(q):
+        return remote(zxsrc.at[q], zxrecv.at[q], zx_s.at[q], zx_r.at[q], device(x, y, zpair, core))
+
     def finish(q):
         own = xs[0] if q % 2 == 1 else ys[0]
         for d in (1, 2, 3):
             direct(q, d).wait_recv()
+
+        def value(h):
+            return (
+                p2[q, own, h].astype(F32) + in2[q, 1, h].astype(F32)
+                + in2[q, 2, h].astype(F32) + in2[q, 3, h].astype(F32)
+            )
+
+        zxsrc[q] = value(1 - zl).astype(BF16)
+        pair_copy(q).start()
+        zown[q] = value(zl)
+
+    def pair_finish(q):
+        pair_copy(q).wait_recv()
+        value = (zown[q] + zxrecv[q].astype(F32)).astype(BF16)
         zsrc = (zsrc0, zsrc1)[q // 2]
-        for h in range(2):
-            value = (
-                p2[q, own, h].astype(F32)
-                + in2[q, 1, h].astype(F32) + in2[q, 2, h].astype(F32) + in2[q, 3, h].astype(F32)
-            ).astype(BF16)
-            for t in range(tiles):
-                zsrc[t * 2 + h, q % 2] = value[:, t * 128 : (t + 1) * 128]
+        for t in range(tiles):
+            zsrc[t, q % 2] = value[:, t * 128 : (t + 1) * 128]
+
+    def z_there(d):
+        there = lax.rem(zh + d, tiles)
+        return there, device(x, y, there * 2 + zl, core)
 
     def z_copy(b, d):
-        there = lax.rem(z + d, nz)
+        there, where = z_there(d)
         src, dst = ((zsrc0, zrecv0), (zsrc1, zrecv1))[b]
-        n = b * nz + d
-        return remote(src.at[there], dst.at[d], z_s.at[n], z_r.at[n], device(x, y, there, core))
+        n = b * tiles + d
+        return remote(src.at[there], dst.at[d], z_s.at[n], z_r.at[n], where)
 
     def zh_copy(d):
-        there = lax.rem(z + d, nz)
-        return remote(zhsrc, zhrecv.at[d], zh_s.at[d], zh_r.at[d], device(x, y, there, core))
+        there, where = z_there(d)
+        return remote(zhsrc.at[there], zhrecv.at[d], zh_s.at[d], zh_r.at[d], where)
 
     def z_send(b):
-        @pl.loop(1, nz)
+        @pl.loop(1, tiles)
         def _(d):
             z_copy(b, d).start()
 
@@ -347,65 +363,79 @@
         hx[0] = hbuf[x] + hx[1] + hx[2] + hx[3]
         hc_copy.start()
 
+    hz_copy = remote(hpair.at[0], hpair.at[1], hz_s, hz_r, device(x, y, zpair, core))
+
+    def gain_pair():
+        hc_copy.wait_recv()
+        hpair[0] = hx[0, yh] + hcross[...]
+        hz_copy.start()
+
     def gain_z():
-        hc_copy.wait_recv()
-        zhsrc[...] = hx[0, yh] + hcross[...]
-
-        @pl.loop(1, nz)
+        hz_copy.wait_recv()
+        both = hpair[0] + hpair[1]
+        for t in range(tiles):
+            zhsrc[t] = both[t : t + 1]
+
+        @pl.loop(1, tiles)
         def _(d):
             zh_copy(d).start()
 
-    from_x(0)
     combine(0)
     ring_open(0)
+    combine(1)
+    ring_open(1)
+    from_x(0)
     from_x(1)
     agc(3).start()
     agc(1).start()
-    combine(1)
-    ring_open(1)
-    from_cross(0)
     combine(2)
     combine(3)
+    from_cross(0)
     hear(1)
     tell(2)
     ring_relay(0)
     ring_relay(1)
     from_opposite()
+    from_cross(3)
+    from_cross(1)
+    from_same(0)
+    ring_close(0)
+    ring_close(1)
     ring_open(2)
     ring_open(3)
-    for d in (3, 1):
-        from_cross(d)
-    from_same(0)
+    from_cross(2)
+    from_same(3)
+    from_same(1)
+    from_same(2)
     ring_relay(2)
     ring_relay(3)
-    from_cross(2)
-    for d in (3, 1):
-        from_same(d)
-    ring_close(0)
-    ring_close(1)
-    from_same(2)
     hear(2)
+    finish(0)
+    finish(1)
+    gain_start()
+    pair_finish(0)
+    pair_finish(1)
+    z_send(0)
     ring_close(2)
     ring_close(3)
-    finish(0)
-    finish(1)
-    z_send(0)
+    gain_cross()
     finish(2)
     finish(3)
+    gain_pair()
+    pair_finish(2)
+    pair_finish(3)
     z_send(1)
-    gain_start()
-    gain_cross()
     gain_z()
 
     mine = yl * 2 + zl
-    fin[mine, 0:2] = zsrc0[z].astype(F32)
-    fin[mine, 2:4] = zsrc1[z].astype(F32)
-    fin[mine, 4, 0:8] = zhsrc[...]
-    fin[mine, 4, 8:16] = jnp.zeros((8, 128), F32)
+    fin[mine, 0:2] = zsrc0[zh].astype(F32)
+    fin[mine, 2:4] = zsrc1[zh].astype(F32)
+    fin[mine, 4] = jnp.zeros((16, 128), F32)
+    fin[mine, 4, 0:1] = zhsrc[zh]
 
     for b in range(2):
 
-        @pl.loop(1, nz)
+        @pl.loop(1, tiles)
         def _(d):
             z_copy(b, d).wait_recv()
             if b == 0:
@@ -413,10 +443,10 @@
             else:
                 fin[mine, 2:4] += zrecv1[d].astype(F32)
 
-    @pl.loop(1, nz)
+    @pl.loop(1, tiles)
     def _(d):
         zh_copy(d).wait_recv()
-        fin[mine, 4, 0:8] += zhrecv[d]
+        fin[mine, 4, 0:1] += zhrecv[d]
 
     ends = [device(x, y, zpair, core), device(x, ysame, z, core), device(x, ysame, zpair, core)]
     fin_copies = [
@@ -446,13 +476,17 @@
         for d in range(1, 4):
             direct(q, d).wait_send()
 
+    for q in range(4):
+        pair_copy(q).wait_send()
+    hz_copy.wait_send()
+
     for b in range(2):
 
-        @pl.loop(1, nz)
+        @pl.loop(1, tiles)
         def _(d):
             z_copy(b, d).wait_send()
 
-    @pl.loop(1, nz)
+    @pl.loop(1, tiles)
     def _(d):
         zh_copy(d).wait_send()
 
@@ -463,9 +497,8 @@
         block = fin[:, q].reshape(64, 128)
         outt[:, q * 64 : (q + 1) * 64] = block.T
     gw_ref[...] = outt[pl.ds(pl.multiple_of(place * 32, 32), 32), :]
-    both = fin[mine, 4] + fin[(1 - yl) * 2 + zl, 4]
-    hrow[...] = pltpu.roll(both[0:8], lax.rem(128 - place * 32, 128), 1)
-    gg_ref[...] = hrow[pl.ds(zh, 1), 0:32]
+    row = fin[mine, 4, 0:8] + fin[(1 - yl) * 2 + zl, 4, 0:8]
+    gg_ref[...] = pltpu.roll(row, lax.rem(128 - place * 32, 128), 1)[0:1, 0:32]
 
 
 def body(tokens, cotangent, weight, gain, exponents):
@@ -496,21 +529,25 @@
         vmem((4, 2, 8, 128), F32),
         vmem((4, 2, 8, 128), F32),
         vmem((8, 128), F32),
-        vmem((nz, 2, 16, 128), BF16),
-        vmem((nz, 2, 16, 128), BF16),
-        vmem((nz, 2, 16, 128), BF16),
-        vmem((nz, 2, 16, 128), BF16),
-        vmem((8, 128), F32),
-        vmem((nz, 8, 128), F32),
+        vmem((2, 8, 128), F32),
+        vmem((4, 16, slab), BF16),
+        vmem((4, 16, slab), BF16),
+        vmem((4, 16, slab), F32),
+        vmem((slab // 128, 2, 16, 128), BF16),
+        vmem((slab // 128, 2, 16, 128), BF16),
+        vmem((slab // 128, 2, 16, 128), BF16),
+        vmem((slab // 128, 2, 16, 128), BF16),
+        vmem((slab // 128, 1, 128), F32),
+        vmem((slab // 128, 1, 128), F32),
         vmem((4, 5, 16, 128), F32),
         vmem((128, 256), F32),
-        vmem((8, 128), F32),
         pltpu.SemaphoreType.REGULAR((3,)),
         dma((4,)), dma((16,)), dma((4,)), dma((4,)), dma, dma,
         dma((4,)), dma((4,)), dma((2,)), dma((2,)), dma((4,)), dma((4,)), dma((4,)), dma((4,)),
         dma((16,)), dma((16,)),
         dma((24,)), dma((24,)), dma((16,)), dma((16,)), dma((4,)), dma((4,)), dma, dma,
-        dma((2 * nz,)), dma((2 * nz,)), dma((nz,)), dma((nz,)), dma((3,)), dma((3,)),
+        dma, dma, dma((4,)), dma((4,)),
+        dma((slab // 64,)), dma((slab // 64,)), dma((slab // 128,)), dma((slab // 128,)), dma((3,)), dma((3,)),
     ]
     any_space = pl.BlockSpec(memory_space=pl.ANY)
     grad_weight, grad_gain = pl.pallas_call(

time: 91.5 us -> 85.6 us (0.936)
  the two profiles are of different devices: /device:TPU:64 before, /device:TPU:8 now
where the time goes in v3:
time: 85.6 us; the launch traced here: 85.4 us
  Pallas kernels  80.7 us (94%)
  local copies, waits for them, and re-layouts  3.98 us (5%)
    pallas_call x1, Pallas kernels, body(): pl.pallas_call(functools.partial(kernel, width, slab, nz), out_shape=(jax...  80.7 us
    unnamed x2, local copies, waits for them, and re-layouts  2.57 us

profile of v3, /device:TPU:8, one launch (start us, length us, event | category | flops | bytes accessed | tf_op | source)
XLA Modules:
  0.0 85.4 jit_solution(17852430277070333240)
XLA Ops:
  0.6 1.4 %reshape.13.gain_hbm = bf16[1,16384]{1,0:T(2,128)(2,1)} reshape(bf16[16384]{0:T(1024)(128)(2,1)} %param.8) | data formatting | bytes 65536 | tf_op jit(solution)/shard_map/reshape | solution.py:565
  2.0 80.7 %shard_map.68 = (f32[32,256]{1,0:T(8,128)}, f32[1,32]{1,0:T(1,128)}) custom-call(bf16[128,16384]{1,0:T(8,128)(2,1)} %tok_hbm.1, bf16[128,256]{1,0:T(8,128)(2,1)} %cot_hbm.1, bf16[1024,256]{1,0:T(8,128)(2,1)} %w_hbm.1, bf16[1,16384]{1,0:T(2,128)(2,1)} %reshape.13.gain_hbm, s32[2,16384]{1,0:T(2,128)} %bitcast.2), custom_call_target="tpu_custom_call" | custom-call | tf_op jit(solution)/shard_map/pallas_call | solution.py:553
  82.8 1.4 %copy.9 = f32[32,256]{1,0:T(8,128)} copy(f32[32,256]{1,0:T(8,128)} %get-tuple-element.8) | data formatting | bytes 65536
  84.2 1.2 %copy.10 = f32[32]{0:T(128)} copy(f32[32]{0:T(128)} %bitcast.3) | data formatting | bytes 256

commit v4 on v3

--- a/solution.py
+++ b/solution.py
@@ -171,10 +171,13 @@
     invb[...] = jnp.broadcast_to(inverse, (128, step))
     cot_t = cotv[...].astype(F32).T.astype(BF16)
 
+    def gain_row(at, size):
+        return gainv[pl.ds(pl.multiple_of(at, size), size)].astype(F32).reshape(1, size)
+
     def partial_slab(i, parity, out):
         s = i * 2 + parity
         for t in range(slab // step):
-            g = gainv[:, pl.ds(pl.multiple_of(s * slab + t * step, step), step)].astype(F32)
+            g = gain_row(s * slab + t * step, step)
             v = tokv[s, :, t * step : (t + 1) * step].astype(F32)
             normed = (v * invb[...] * g).astype(BF16)
             part = jnp.dot(cot_t, normed, preferred_element_type=F32)
@@ -186,9 +189,12 @@
 
     exps = remote(expv, sibexp, exp_s, exp_r, sibling)
 
-    @pl.loop(0, 8)
+    @pl.loop(0, 2)
     def _(i):
-        partial_slab(i, 1 - core, usend)
+        partial_slab(i * 4, 1 - core, usend)
+        partial_slab(i * 4 + 1, 1 - core, usend)
+        partial_slab(i * 4 + 2, 1 - core, usend)
+        partial_slab(i * 4 + 3, 1 - core, usend)
 
     pl.semaphore_wait(barrier, len(partners))
     tell(0)
@@ -203,9 +209,12 @@
     core_copy(2).start()
     core_copy(3).start()
 
-    @pl.loop(0, 8)
+    @pl.loop(0, 2)
     def _(i):
-        partial_slab(i, core, uown)
+        partial_slab(i * 4, core, uown)
+        partial_slab(i * 4 + 1, core, uown)
+        partial_slab(i * 4 + 2, core, uown)
+        partial_slab(i * 4 + 3, core, uown)
 
     hear(0)
     tell(1)
@@ -293,7 +302,7 @@
                 u = uown[i, g].astype(F32) + urecv[i, g].astype(F32)
                 total = total + u * wall[px, pyh, g].astype(F32)
             at = pl.multiple_of(i * 2 * slab + parity_at, slab)
-            row = jnp.sum(total, axis=0, keepdims=True) / gainv[:, pl.ds(at, slab)].astype(F32)
+            row = jnp.sum(total, axis=0, keepdims=True) / gain_row(at, slab)
             if tiles < 8:
                 hbuf[px, pyh] = jnp.zeros((8, 128), F32)
             for t in range(tiles):
@@ -501,6 +510,17 @@
     gg_ref[...] = pltpu.roll(row, lax.rem(128 - place * 32, 128), 1)[0:1, 0:32]
 
 
+def hand_over(gw_ref, gg_ref, gw_out, gg_out, sem):
+    copies = [
+        pltpu.make_async_copy(gw_ref, gw_out, sem.at[0]),
+        pltpu.make_async_copy(gg_ref, gg_out, sem.at[1]),
+    ]
+    for copy in copies:
+        copy.start()
+    for copy in copies:
+        copy.wait()
+
+
 def body(tokens, cotangent, weight, gain, exponents):
     width = tokens.shape[1]
     nz = lax.axis_size("rep") // 2
@@ -511,7 +531,7 @@
         vmem((16, 128, slab), BF16),
         vmem((128, 256), BF16),
         vmem((slab, 256), BF16),
-        vmem((1, width), BF16),
+        vmem((width,), BF16),
         vmem((2, width), jnp.int32),
         vmem((2, width), jnp.int32),
         vmem((128, min(slab, 256)), F32),
@@ -562,7 +582,18 @@
         compiler_params=pltpu.CompilerParams(
             collective_id=0, has_side_effects=True, vmem_limit_bytes=60 * 2**20
         ),
-    )(tokens, cotangent, weight, gain.reshape(1, width), exponents.reshape(2, width))
+    )(tokens, cotangent, weight, gain, exponents.reshape(2, width))
+    grad_weight, grad_gain = pl.pallas_call(
+        hand_over,
+        out_shape=(
+            jax.ShapeDtypeStruct((32, 256), F32),
+            jax.ShapeDtypeStruct((1, 32), F32),
+        ),
+        in_specs=[any_space] * 2,
+        out_specs=(any_space,) * 2,
+        scratch_shapes=[dma((2,))],
+        compiler_params=pltpu.CompilerParams(vmem_limit_bytes=60 * 2**20),
+    )(grad_weight, grad_gain)
     return (grad_weight, grad_gain.reshape(32))
 
 

time: 85.6 us -> 82.6 us (0.965)
  local copies, waits for them, and re-layouts: 3.98 us -> 0 us
  Pallas kernels: 80.7 us -> 81.8 us
    unnamed x2 -> x0, local copies, waits for them, and re-layouts: 2.57 us -> none
    pallas_call x0 -> x1, Pallas kernels: none -> 2.13 us  [body(): pl.pallas_call(hand_over, out_shape=(jax.ShapeDtypeStruct((32, 256), F32)...]
    reshape x1 -> x0, local copies, waits for them, and re-layouts: 1.41 us -> none  [body(): gain.reshape(1, width)]
    pallas_call x1, Pallas kernels: 80.7 us -> 79.7 us  [body(): pl.pallas_call(functools.partial(kernel, width, slab, nz), out_shape=(jax...]
where the time goes in v4:
time: 82.6 us; the launch traced here: 82.5 us
  Pallas kernels  81.8 us (99%)
    pallas_call x1, Pallas kernels, body(): pl.pallas_call(functools.partial(kernel, width, slab, nz), out_shape=(jax...  79.7 us
    pallas_call x1, Pallas kernels, body(): pl.pallas_call(hand_over, out_shape=(jax.ShapeDtypeStruct((32, 256), F32)...  2.13 us

profile of v4, /device:TPU:8, one launch (start us, length us, event | category | flops | bytes accessed | tf_op | source)
XLA Modules:
  0.0 82.5 jit_solution(2510007141603544399)
XLA Ops:
  0.6 79.7 %shard_map.68 = (f32[32,256]{1,0:T(8,128)}, f32[1,32]{1,0:T(1,128)}) custom-call(bf16[128,16384]{1,0:T(8,128)(2,1)} %tok_hbm.1, bf16[128,256]{1,0:T(8,128)(2,1)} %cot_hbm.1, bf16[1024,256]{1,0:T(8,128)(2,1)} %w_hbm.1, bf16[16384]{0:T(1024)(128)(2,1)} %gain_hbm.1, s32[2,16384]{1,0:T(2,128)} %bitcast.2), custom_call_target="tpu_custom_call" | custom-call | tf_op jit(solution)/shard_map/pallas_call | solution.py:573
  80.3 2.1 %shard_map.69 = (f32[32,256]{1,0:T(8,128)}, f32[1,32]{1,0:T(1,128)}) custom-call(f32[32,256]{1,0:T(8,128)} %get-tuple-element.6.gw_ref, f32[1,32]{1,0:T(1,128)} %get-tuple-element.7.gg_ref), custom_call_target="tpu_custom_call" | custom-call | tf_op jit(solution)/shard_map/pallas_call | solution.py:586

commit v5 on v4

--- a/solution.py
+++ b/solution.py
@@ -436,34 +436,6 @@
     z_send(1)
     gain_z()
 
-    mine = yl * 2 + zl
-    fin[mine, 0:2] = zsrc0[zh].astype(F32)
-    fin[mine, 2:4] = zsrc1[zh].astype(F32)
-    fin[mine, 4] = jnp.zeros((16, 128), F32)
-    fin[mine, 4, 0:1] = zhsrc[zh]
-
-    for b in range(2):
-
-        @pl.loop(1, tiles)
-        def _(d):
-            z_copy(b, d).wait_recv()
-            if b == 0:
-                fin[mine, 0:2] += zrecv0[d].astype(F32)
-            else:
-                fin[mine, 2:4] += zrecv1[d].astype(F32)
-
-    @pl.loop(1, tiles)
-    def _(d):
-        zh_copy(d).wait_recv()
-        fin[mine, 4, 0:1] += zhrecv[d]
-
-    ends = [device(x, y, zpair, core), device(x, ysame, z, core), device(x, ysame, zpair, core)]
-    fin_copies = [
-        remote(fin.at[mine], fin.at[mine], fin_s.at[k], fin_r.at[k], ends[k]) for k in range(3)
-    ]
-    for copy in fin_copies:
-        copy.start()
-
     for d in range(1, 4):
         hx_copy(d).wait_send()
     for k in range(2):
@@ -488,6 +460,34 @@
     for q in range(4):
         pair_copy(q).wait_send()
     hz_copy.wait_send()
+
+    mine = yl * 2 + zl
+    fin[mine, 0:2] = zsrc0[zh].astype(F32)
+    fin[mine, 2:4] = zsrc1[zh].astype(F32)
+    fin[mine, 4] = jnp.zeros((16, 128), F32)
+    fin[mine, 4, 0:1] = zhsrc[zh]
+
+    for b in range(2):
+
+        @pl.loop(1, tiles)
+        def _(d):
+            z_copy(b, d).wait_recv()
+            if b == 0:
+                fin[mine, 0:2] += zrecv0[d].astype(F32)
+            else:
+                fin[mine, 2:4] += zrecv1[d].astype(F32)
+
+    @pl.loop(1, tiles)
+    def _(d):
+        zh_copy(d).wait_recv()
+        fin[mine, 4, 0:1] += zhrecv[d]
+
+    ends = [device(x, y, zpair, core), device(x, ysame, z, core), device(x, ysame, zpair, core)]
+    fin_copies = [
+        remote(fin.at[mine], fin.at[mine], fin_s.at[k], fin_r.at[k], ends[k]) for k in range(3)
+    ]
+    for copy in fin_copies:
+        copy.start()
 
     for b in range(2):
 

time: 82.6 us -> 82.6 us (level)
  no operation moved by 1% of the time
where the time goes in v5:
time: 82.6 us; the launch traced here: 82.5 us
  Pallas kernels  81.8 us (99%)
    pallas_call x1, Pallas kernels, body(): pl.pallas_call(functools.partial(kernel, width, slab, nz), out_shape=(jax...  79.7 us
    pallas_call x1, Pallas kernels, body(): pl.pallas_call(hand_over, out_shape=(jax.ShapeDtypeStruct((32, 256), F32)...  2.13 us

profile of v5, /device:TPU:8, one launch (start us, length us, event | category | flops | bytes accessed | tf_op | source)
XLA Modules:
  0.0 82.5 jit_solution(16967725746923689320)
XLA Ops:
  0.6 79.7 %shard_map.68 = (f32[32,256]{1,0:T(8,128)}, f32[1,32]{1,0:T(1,128)}) custom-call(bf16[128,16384]{1,0:T(8,128)(2,1)} %tok_hbm.1, bf16[128,256]{1,0:T(8,128)(2,1)} %cot_hbm.1, bf16[1024,256]{1,0:T(8,128)(2,1)} %w_hbm.1, bf16[16384]{0:T(1024)(128)(2,1)} %gain_hbm.1, s32[2,16384]{1,0:T(2,128)} %bitcast.2), custom_call_target="tpu_custom_call" | custom-call | tf_op jit(solution)/shard_map/pallas_call | solution.py:573
  80.3 2.1 %shard_map.69 = (f32[32,256]{1,0:T(8,128)}, f32[1,32]{1,0:T(1,128)}) custom-call(f32[32,256]{1,0:T(8,128)} %get-tuple-element.6.gw_ref, f32[1,32]{1,0:T(1,128)} %get-tuple-element.7.gg_ref), custom_call_target="tpu_custom_call" | custom-call | tf_op jit(solution)/shard_map/pallas_call | solution.py:586
